TPU v7x, 256 devices: a whole 4x4x8 slice. The times are simulated.
256 devices in a mesh: slab: 8 (over x, core), pos: 32 (over y, z).
Axes of the slice: x: 4, y: 4, z: 8, core: 2. Of those that a mesh axis runs over, the one named last changes fastest.
Arguments:
- object_field: float32 [2, 8, 4096, 2048], P(None, 'slab', 'pos'), may hold values from -0.25 to 1.15, as said below
- probe_wave: float32 [2, 128, 128], replicated, may hold values from -4.2 to 4.2
- scan_coords: int32 [96, 2], P('pos'), may hold values from 0 to 3968, as said below
- scan_counts: int32 [32], P('pos'), may hold values from 1 to 3, as said below
- measured: float32 [96, 128, 128], P('pos'), may hold values from 0.1 to 3
Outputs:
- object_gradient: float32 [2, 8, 4096, 2048], P(None, 'slab', 'pos')
Inputs may be any that keep to these rules, and one draw needn't show every extreme that they name: `object_field`: real parts between 0.85 and 1.15, imaginary parts between -0.25 and 0.25. `scan_coords`: slot q belongs to owner j = q div 3; its row corner lies in [j * 128, (j + 1) * 128) and is at most 3968; its column corner is at most 1920. The first scan_counts[j] slots of owner j are live, the others are not; some owner has all 3 live.
All inputs are finite; a program needn't handle non-finite values.
Results may differ from a plain program's by a relative error of at most 0.02.
Values may be sent and summed in bfloat16 or wider, within the bound.
A program may use at most 64 MiB of HBM per device.

v0:
```python
import jax
import jax.numpy as jnp
import numpy as np
from jax import lax
from jax.experimental import pallas as pl
from jax.experimental.pallas import tpu as pltpu
from jax.sharding import PartitionSpec as P

f32 = jnp.float32
bf16 = jnp.bfloat16
N = 128
SLICES = 8
CAP = 3
N_POS = 32
NCOL = 2048
WORKERS = (0, 2, 6)
MESH = pl.DeviceIdType.MESH


def split_bf16(values):
    high = np.asarray(values, np.float32).astype(jnp.bfloat16)
    low = (values - high.astype(np.float64)).astype(np.float32).astype(jnp.bfloat16)
    return high, low


def tables():
    j = np.arange(N)
    fourier = np.exp(-2j * np.pi * ((j[:, None] * j) % N) / N) / np.sqrt(N)
    centred = (j + N // 2) % N - N // 2
    phase = np.exp(-0.5j * centred * centred / N)
    step = fourier.conj() @ (phase[:, None] * fourier)
    out = []
    for matrix in (step, fourier):
        real_high, real_low = split_bf16(matrix.real)
        imag_high, imag_low = split_bf16(matrix.imag)
        out.append(np.block([[real_high, real_low], [imag_high, imag_low]]))
        out.append(np.block([[real_high, imag_high], [real_low, imag_low]]))
    return np.stack(out)


def sandwich(left, right, real, imag, sign):
    x = jnp.concatenate([real.astype(bf16), imag.astype(bf16)], axis=1)
    x = jnp.concatenate([x, x], axis=0)
    y = jnp.dot(left, x, preferred_element_type=f32)
    if sign > 0:
        real, imag = y[:N, :N] - y[N:, N:], y[:N, N:] + y[N:, :N]
    else:
        real, imag = y[:N, :N] + y[N:, N:], y[:N, N:] - y[N:, :N]
    x = jnp.concatenate([real.astype(bf16), imag.astype(bf16)], axis=0)
    x = jnp.concatenate([x, x], axis=1)
    y = jnp.dot(x, right, preferred_element_type=f32)
    if sign > 0:
        return y[:N, :N] - y[N:, N:], y[:N, N:] + y[N:, :N]
    return y[:N, :N] + y[N:, N:], y[N:, :N] - y[:N, N:]


def corner(coords, k, strip):
    row = coords[k, 0] - strip * N
    col = coords[k, 1]
    block = jnp.minimum(lax.shift_right_arithmetic(col, 7), NCOL // N - 2)
    return row, block, col - block * N


def gather_kernel(
    coords_ref, counts_ref, object_ref, probe_ref, measured_ref, tables_ref,
    grads_ref, info_ref,
    strip, probe, table, sample, live, live_in, coords_in,
    top_out, low_out, tops, lows, kept, grad_out,
    block_sem, load_sem, coord_sem, sample_sem, live_sem,
    top_send, top_recv, low_send, low_recv, grad_send, grad_recv, own_sem,
):
    s = lax.axis_index("slab")
    p = lax.axis_index("pos")
    after = lax.rem(p + 1, N_POS)
    before = lax.rem(p + N_POS - 1, N_POS)
    is_worker = (s == WORKERS[0]) | (s == WORKERS[1]) | (s == WORKERS[2])
    slot = s // 2 - s // 6

    def load_block(c):
        columns = pl.ds(pl.multiple_of(c * N, N), N)
        return pltpu.make_async_copy(object_ref.at[:, 0, :, columns], strip.at[c], block_sem.at[c])

    def start_block(c, carry):
        load_block(c).start()
        return carry

    def wait_block(c, carry):
        load_block(c).wait()
        return carry

    lax.fori_loop(0, NCOL // N, start_block, 0)
    load_probe = pltpu.make_async_copy(probe_ref, probe, load_sem.at[1])
    load_table = pltpu.make_async_copy(tables_ref, table, load_sem.at[2])

    barrier = pltpu.get_barrier_semaphore()

    def greet(where):
        pl.semaphore_signal(barrier, inc=1, device_id=where, device_id_type=MESH)

    greet((s, after))
    greet((s, before))
    for w in WORKERS:
        greet((w, after))

        @pl.when(s != w)
        def _():
            greet((w, p))

    @pl.when(is_worker)
    def _():
        load_probe.start()
        load_table.start()
        for other in range(SLICES):
            greet((other, before))

            @pl.when(s != other)
            def _():
                greet((other, p))

    @pl.when(is_worker)
    def _():
        pl.semaphore_wait(barrier, 22)

    @pl.when(jnp.logical_not(is_worker))
    def _():
        pl.semaphore_wait(barrier, 8)

    def send(src, dst, send_sem, recv_sem, where):
        return pltpu.make_async_remote_copy(
            src_ref=src, dst_ref=dst, send_sem=send_sem, recv_sem=recv_sem,
            device_id=where, device_id_type=MESH,
        )

    coord_copy = send(coords_ref, coords_in, coord_sem.at[0], coord_sem.at[1], (s, after))
    coord_copy.start()

    def sample_copy(k):
        return send(measured_ref.at[k], sample, sample_sem.at[0], sample_sem.at[1], (s, after))

    live_copy = send(live, live_in, live_sem.at[0], live_sem.at[1], (s, after))
    for k, w in enumerate(WORKERS):

        @pl.when(s == w)
        def _():
            sample_copy(k).start()
            live[...] = jnp.clip(jnp.full((8, N), counts_ref[0] - k, jnp.int32), 0, 1).astype(f32)
            live_copy.start()

    row_id = lax.broadcasted_iota(jnp.int32, (N, N), 0)
    lane_id = lax.broadcasted_iota(jnp.int32, (N, N), 1)
    window_row = lax.broadcasted_iota(jnp.int32, (2 * N, N), 0)
    window_lane = lax.broadcasted_iota(jnp.int32, (2 * N, N), 1)

    def one_hot(where):
        return jnp.where(where, 1.0, 0.0).astype(bf16)

    def cut(first_row, block, shift, dst, k):
        near = strip[block]
        far = strip[block + 1]
        real = jnp.concatenate([near[0] - 1.0, far[0] - 1.0], axis=1)
        imag = jnp.concatenate([near[1], far[1]], axis=1)
        window = jnp.concatenate([real.astype(bf16), imag.astype(bf16)], axis=0)
        moved = one_hot(window_row == window_lane + shift)
        tile = jnp.dot(window, moved, preferred_element_type=f32).astype(bf16)
        tile = jnp.concatenate([tile[:N], tile[N:]], axis=1)
        moved = one_hot(lane_id == row_id + first_row)
        tile = jnp.dot(moved, tile, preferred_element_type=f32).astype(bf16)
        dst[k, 0] = tile[:, :N]
        dst[k, 1] = tile[:, N:]

    lax.fori_loop(0, NCOL // N, wait_block, 0)
    own = coords_ref[...]
    for k, w in enumerate(WORKERS):
        row, block, shift = corner(own, k, p)
        cut(row, block, shift, top_out, k)
        send(top_out.at[k], tops.at[s], top_send.at[k], top_recv.at[s], (w, after)).start()

    coord_copy.wait_recv()
    theirs = coords_in[...]
    info_ref[0] = own
    info_ref[1] = theirs
    for k, w in enumerate(WORKERS):
        row, block, shift = corner(theirs, k, before)
        cut(row - N, block, shift, low_out, k)

        @pl.when(s != w)
        def _():
            send(low_out.at[k], lows.at[s], low_send.at[k], low_recv.at[s], (w, p)).start()

        @pl.when(s == w)
        def _():
            lows[s] = low_out[k]

    @pl.when(is_worker)
    def _():
        load_probe.wait()
        load_table.wait()

        def patch(i):
            return (
                tops[i, 0].astype(f32) + lows[i, 0].astype(f32),
                tops[i, 1].astype(f32) + lows[i, 1].astype(f32),
            )

        def arrive(i):
            send(top_out.at[0], tops.at[i], top_send.at[0], top_recv.at[i], (s, after)).wait_recv()

            @pl.when(i != s)
            def _():
                send(low_out.at[0], lows.at[i], low_send.at[0], low_recv.at[i], (s, p)).wait_recv()

        def through(i, real, imag):
            kept[i, 0] = real
            kept[i, 1] = imag
            arrive(i)
            d_real, d_imag = patch(i)
            return (
                real + (real * d_real - imag * d_imag),
                imag + (real * d_imag + imag * d_real),
            )

        def forward(i, wave):
            return sandwich(table[0], table[1], *through(i, *wave), 1)

        wave = lax.fori_loop(0, SLICES - 1, forward, (probe[0], probe[1]))
        real, imag = sandwich(table[2], table[3], *through(SLICES - 1, *wave), 1)
        sample_copy(0).wait_recv()
        live_copy.wait_recv()
        weight = (real * real + imag * imag - sample[...]) * live_in[0:1, :]
        moved = sandwich(table[2], table[3], weight * real, weight * imag, -1)

        def emit(i, moved):
            real, imag = moved
            grad_out[i, 0] = (kept[i, 0] * real + kept[i, 1] * imag).astype(bf16)
            grad_out[i, 1] = (kept[i, 0] * imag - kept[i, 1] * real).astype(bf16)
            send(
                grad_out.at[i], grads_ref.at[slot], grad_send.at[i, 0], grad_recv.at[slot], (i, before)
            ).start()

            @pl.when(i != s)
            def _():
                send(
                    grad_out.at[i], grads_ref.at[CAP + slot], grad_send.at[i, 1],
                    grad_recv.at[CAP + slot], (i, p),
                ).start()

            @pl.when(i == s)
            def _():
                pltpu.make_async_copy(grad_out.at[i], grads_ref.at[CAP + slot], own_sem).start()

        def backward(step, moved):
            i = SLICES - 1 - step
            emit(i, moved)
            real, imag = moved
            d_real, d_imag = patch(i)
            return sandwich(
                table[0], table[1],
                real + (d_real * real + d_imag * imag),
                imag + (d_real * imag - d_imag * real),
                -1,
            )

        emit(0, lax.fori_loop(0, SLICES - 1, backward, moved))

    for k, w in enumerate(WORKERS):
        here = grad_out.at[0]
        send(here, grads_ref.at[k], grad_send.at[0, 0], grad_recv.at[k], (s, after)).wait_recv()

        @pl.when(s != w)
        def _():
            send(
                here, grads_ref.at[CAP + k], grad_send.at[0, 0], grad_recv.at[CAP + k], (s, after)
            ).wait_recv()
            send(low_out.at[k], lows.at[s], low_send.at[k], low_recv.at[s], (w, p)).wait_send()

        @pl.when(s == w)
        def _():
            pltpu.make_async_copy(here, grads_ref.at[CAP + k], own_sem).wait()
            sample_copy(k).wait_send()
            live_copy.wait_send()

        send(top_out.at[k], tops.at[s], top_send.at[k], top_recv.at[s], (w, after)).wait_send()

    coord_copy.wait_send()

    @pl.when(is_worker)
    def _():
        def drain(i, carry):
            send(grad_out.at[i], grads_ref.at[slot], grad_send.at[i, 0], grad_recv.at[slot], (i, before)).wait_send()

            @pl.when(i != s)
            def _():
                send(
                    grad_out.at[i], grads_ref.at[CAP + slot], grad_send.at[i, 1],
                    grad_recv.at[CAP + slot], (i, p),
                ).wait_send()

            return carry

        lax.fori_loop(0, SLICES, drain, 0)


def scatter_kernel(info_ref, grads_ref, out_ref, total, sem):
    p = lax.axis_index("pos")
    before = lax.rem(p + N_POS - 1, N_POS)
    total[...] = jnp.zeros((2, N, NCOL), f32)
    row_id = lax.broadcasted_iota(jnp.int32, (N, N), 0)
    lane_id = lax.broadcasted_iota(jnp.int32, (N, N), 1)
    for side in range(2):
        coords = info_ref[side]
        for k in range(CAP):
            row, block, shift = corner(coords, k, p if side == 0 else before)
            keep = row_id >= row if side == 0 else row_id < row
            base = pl.multiple_of(block * N, N)
            near = pl.ds(base, N)
            far = pl.ds(pl.multiple_of(base + N, N), N)
            turn = lax.rem(shift, N)
            for part in range(2):
                tile = pltpu.roll(grads_ref[side * CAP + k, part].astype(f32), turn, 1)
                tile = jnp.where(keep, pltpu.roll(tile, row, 0), 0.0)
                total[part, :, near] += jnp.where(lane_id >= shift, tile, 0.0)
                total[part, :, far] += jnp.where(lane_id < shift, tile, 0.0)
    store = pltpu.make_async_copy(total, out_ref.at[:, 0], sem)
    store.start()
    store.wait()


def per_device(object_field, probe_wave, scan_coords, scan_counts, measured):
    vmem = pl.BlockSpec(memory_space=pltpu.VMEM)
    smem = pl.BlockSpec(memory_space=pltpu.SMEM)
    anywhere = pl.BlockSpec(memory_space=pl.ANY)
    hbm = pl.BlockSpec(memory_space=pltpu.HBM)
    dma = pltpu.SemaphoreType.DMA
    grads, info = pl.pallas_call(
        gather_kernel,
        out_shape=(
            jax.ShapeDtypeStruct((2 * CAP, 2, N, N), bf16),
            jax.ShapeDtypeStruct((2, CAP, 2), jnp.int32),
        ),
        in_specs=[vmem, smem, hbm, hbm, hbm, hbm],
        out_specs=(anywhere, vmem),
        scratch_shapes=[
            pltpu.VMEM((NCOL // N, 2, N, N), f32),
            pltpu.VMEM((2, N, N), f32),
            pltpu.VMEM((4, 2 * N, 2 * N), bf16),
            pltpu.VMEM((N, N), f32),
            pltpu.VMEM((8, N), f32),
            pltpu.VMEM((8, N), f32),
            pltpu.VMEM((CAP, 2), jnp.int32),
            pltpu.VMEM((CAP, 2, N, N), bf16),
            pltpu.VMEM((CAP, 2, N, N), bf16),
            pltpu.VMEM((SLICES, 2, N, N), bf16),
            pltpu.VMEM((SLICES, 2, N, N), bf16),
            pltpu.VMEM((SLICES, 2, N, N), f32),
            pltpu.VMEM((SLICES, 2, N, N), bf16),
            dma((NCOL // N,)), dma((3,)), dma((2,)), dma((2,)), dma((2,)),
            dma((CAP,)), dma((SLICES,)), dma((CAP,)), dma((SLICES,)),
            dma((SLICES, 2)), dma((2 * CAP,)), dma,
        ],
        compiler_params=pltpu.CompilerParams(
            collective_id=0, has_side_effects=True, vmem_limit_bytes=60 << 20
        ),
        name="chain",
    )(scan_coords, scan_counts, object_field, probe_wave, measured, jnp.asarray(tables()))
    return pl.pallas_call(
        scatter_kernel,
        out_shape=jax.ShapeDtypeStruct(object_field.shape, f32),
        in_specs=[vmem, vmem],
        out_specs=anywhere,
        scratch_shapes=[pltpu.VMEM((2, N, NCOL), f32), dma],
        compiler_params=pltpu.CompilerParams(vmem_limit_bytes=40 << 20),
        name="scatter",
    )(info, grads)


def solution(mesh):
    in_specs = (P(None, "slab", "pos", None), P(), P("pos", None), P("pos"), P("pos", None, None))
    out_specs = P(None, "slab", "pos", None)
    return jax.shard_map(
        per_device, mesh=mesh, in_specs=in_specs, out_specs=out_specs, check_vma=False
    )
```

profile of v0, /device:TPU:1, one launch (start us, length us, event | category | flops | bytes accessed | tf_op | source)
XLA Modules:
  0.0 40.6 jit_solution(13398003607406122298)
XLA Ops:
  0.7 1.3 %copy.7.coords_ref = s32[3,2]{1,0:T(4,128)} copy(s32[3,2]{0,1:T(2,128)} %param.8) | data formatting | bytes 48 | tf_op args[2]
  2.0 34.7 %chain.1 = (bf16[6,2,128,128]{3,2,1,0:T(8,128)(2,1)}, s32[2,3,2]{2,1,0:T(4,128)}) custom-call(s32[3,2]{1,0:T(4,128)} %copy.7.coords_ref, s32[1]{0:T(128)S(6)} %copy.8.counts_ref, f32[2,1,128,2048]{3,2,1,0:T(8,128)} %object_ref.1, f32[2,128,128]{2,1,0:T(8,128)} %probe_ref.1, f32[3,128,128]{2,1,0:T(8,128)} %measured_ref.1, ...), custom_call_target="tpu_custom_call" | custom-call | tf_op jit(solution)/shard_map/chain/pallas_call | solution.py:334
  36.7 0.0 copy-start
  36.7 1.0 %copy-done = bf16[6,2,128,128]{3,2,1,0:T(8,128)(2,1)S(1)} copy-done((bf16[6,2,128,128]{3,2,1,0:T(8,128)(2,1)S(1)}, bf16[6,2,128,128]{3,2,1,0:T(8,128)(2,1)}, u32[]{:S(2)}) %copy-start) | copy-done | bytes 393240
  37.7 0.0 copy-start.1
  37.7 0.7 %copy-done.1 = s32[2,3,2]{2,1,0:T(4,128)S(1)} copy-done((s32[2,3,2]{2,1,0:T(4,128)S(1)}, s32[2,3,2]{2,1,0:T(4,128)}, u32[]{:S(2)}) %copy-start.1) | copy-done | bytes 72
  38.4 2.2 %scatter.1 = f32[2,1,128,2048]{3,2,1,0:T(8,128)} custom-call(s32[2,3,2]{2,1,0:T(4,128)S(1)} %copy-done.1, bf16[6,2,128,128]{3,2,1,0:T(8,128)(2,1)S(1)} %copy-done), custom_call_target="tpu_custom_call" | custom-call | tf_op jit(solution)/shard_map/scatter/pallas_call | solution.py:365
Async XLA Ops:
  36.7 1.0 %copy-start = (bf16[6,2,128,128]{3,2,1,0:T(8,128)(2,1)S(1)}, bf16[6,2,128,128]{3,2,1,0:T(8,128)(2,1)}, u32[]{:S(2)}) copy-start(bf16[6,2,128,128]{3,2,1,0:T(8,128)(2,1)} %get-tuple-element.8.grads_ref) | copy-start | bytes 1179652
  37.7 0.7 %copy-start.1 = (s32[2,3,2]{2,1,0:T(4,128)S(1)}, s32[2,3,2]{2,1,0:T(4,128)}, u32[]{:S(2)}) copy-start(s32[2,3,2]{2,1,0:T(4,128)} %get-tuple-element.7.info_ref) | copy-start | bytes 148
where the time goes:
time: 40.9 us; the launch traced here: 40.6 us
  Pallas kernels  36.9 us (90%)
  local copies, waits for them, and re-layouts  3.01 us (7%)
  between operations  0.67 us (2%)
    pallas_call x1, Pallas kernels, per_device(): pl.pallas_call(gather_kernel, out_shape=(jax.ShapeDtypeStruct((2 * CAP, 2...  34.7 us
    unnamed x5, local copies, waits for them, and re-layouts  3.01 us
    pallas_call x1, Pallas kernels, per_device(): pl.pallas_call(scatter_kernel, out_shape=jax.ShapeDtypeStruct(object_fiel...  2.21 us

commit v1 on v0

--- a/solution.py
+++ b/solution.py
@@ -11,7 +11,6 @@
 N = 128
 SLICES = 8
 CAP = 3
-N_POS = 32
 NCOL = 2048
 WORKERS = (0, 2, 6)
 MESH = pl.DeviceIdType.MESH
@@ -55,8 +54,8 @@
 
 
 def corner(coords, k, strip):
-    row = coords[k, 0] - strip * N
-    col = coords[k, 1]
+    row = coords[0, k] - strip * N
+    col = coords[1, k]
     block = jnp.minimum(lax.shift_right_arithmetic(col, 7), NCOL // N - 2)
     return row, block, col - block * N
 
@@ -71,8 +70,9 @@
 ):
     s = lax.axis_index("slab")
     p = lax.axis_index("pos")
-    after = lax.rem(p + 1, N_POS)
-    before = lax.rem(p + N_POS - 1, N_POS)
+    strips = lax.axis_size("pos")
+    after = lax.rem(p + 1, strips)
+    before = lax.rem(p + strips - 1, strips)
     is_worker = (s == WORKERS[0]) | (s == WORKERS[1]) | (s == WORKERS[2])
     slot = s // 2 - s // 6
 
@@ -148,40 +148,30 @@
 
     row_id = lax.broadcasted_iota(jnp.int32, (N, N), 0)
     lane_id = lax.broadcasted_iota(jnp.int32, (N, N), 1)
-    window_row = lax.broadcasted_iota(jnp.int32, (2 * N, N), 0)
-    window_lane = lax.broadcasted_iota(jnp.int32, (2 * N, N), 1)
-
-    def one_hot(where):
-        return jnp.where(where, 1.0, 0.0).astype(bf16)
-
-    def cut(first_row, block, shift, dst, k):
+
+    def cut(keep, block, shift, dst, k):
         near = strip[block]
         far = strip[block + 1]
-        real = jnp.concatenate([near[0] - 1.0, far[0] - 1.0], axis=1)
-        imag = jnp.concatenate([near[1], far[1]], axis=1)
-        window = jnp.concatenate([real.astype(bf16), imag.astype(bf16)], axis=0)
-        moved = one_hot(window_row == window_lane + shift)
-        tile = jnp.dot(window, moved, preferred_element_type=f32).astype(bf16)
-        tile = jnp.concatenate([tile[:N], tile[N:]], axis=1)
-        moved = one_hot(lane_id == row_id + first_row)
-        tile = jnp.dot(moved, tile, preferred_element_type=f32).astype(bf16)
-        dst[k, 0] = tile[:, :N]
-        dst[k, 1] = tile[:, N:]
+        for part in range(2):
+            tile = jnp.where(lane_id >= shift, near[part], far[part])
+            if part == 0:
+                tile = tile - 1.0
+            dst[k, part] = jnp.where(keep, tile, 0.0).astype(bf16)
 
     lax.fori_loop(0, NCOL // N, wait_block, 0)
     own = coords_ref[...]
     for k, w in enumerate(WORKERS):
         row, block, shift = corner(own, k, p)
-        cut(row, block, shift, top_out, k)
+        cut(row_id >= row, block, shift, top_out, k)
         send(top_out.at[k], tops.at[s], top_send.at[k], top_recv.at[s], (w, after)).start()
 
     coord_copy.wait_recv()
     theirs = coords_in[...]
-    info_ref[0] = own
-    info_ref[1] = theirs
+    info_ref[...] = theirs
+    corners = [corner(theirs, k, before) for k in range(CAP)]
     for k, w in enumerate(WORKERS):
-        row, block, shift = corner(theirs, k, before)
-        cut(row - N, block, shift, low_out, k)
+        row, block, shift = corners[k]
+        cut(row_id < row, block, shift, low_out, k)
 
         @pl.when(s != w)
         def _():
@@ -222,7 +212,13 @@
         def forward(i, wave):
             return sandwich(table[0], table[1], *through(i, *wave), 1)
 
-        wave = lax.fori_loop(0, SLICES - 1, forward, (probe[0], probe[1]))
+        row = jnp.where(slot == 0, corners[0][0], jnp.where(slot == 1, corners[1][0], corners[2][0]))
+        shift = jnp.where(slot == 0, corners[0][2], jnp.where(slot == 1, corners[1][2], corners[2][2]))
+
+        def turned(x):
+            return pltpu.roll(pltpu.roll(x, lax.rem(shift, N), 1), row, 0)
+
+        wave = lax.fori_loop(0, SLICES - 1, forward, (turned(probe[0]), turned(probe[1])))
         real, imag = sandwich(table[2], table[3], *through(SLICES - 1, *wave), 1)
         sample_copy(0).wait_recv()
         live_copy.wait_recv()
@@ -300,24 +296,22 @@
         lax.fori_loop(0, SLICES, drain, 0)
 
 
-def scatter_kernel(info_ref, grads_ref, out_ref, total, sem):
+def scatter_kernel(own_ref, their_ref, grads_ref, out_ref, total, sem):
     p = lax.axis_index("pos")
-    before = lax.rem(p + N_POS - 1, N_POS)
+    before = lax.rem(p + lax.axis_size("pos") - 1, lax.axis_size("pos"))
     total[...] = jnp.zeros((2, N, NCOL), f32)
     row_id = lax.broadcasted_iota(jnp.int32, (N, N), 0)
     lane_id = lax.broadcasted_iota(jnp.int32, (N, N), 1)
     for side in range(2):
-        coords = info_ref[side]
+        coords = own_ref[...] if side == 0 else their_ref[...]
         for k in range(CAP):
             row, block, shift = corner(coords, k, p if side == 0 else before)
             keep = row_id >= row if side == 0 else row_id < row
             base = pl.multiple_of(block * N, N)
             near = pl.ds(base, N)
             far = pl.ds(pl.multiple_of(base + N, N), N)
-            turn = lax.rem(shift, N)
             for part in range(2):
-                tile = pltpu.roll(grads_ref[side * CAP + k, part].astype(f32), turn, 1)
-                tile = jnp.where(keep, pltpu.roll(tile, row, 0), 0.0)
+                tile = jnp.where(keep, grads_ref[side * CAP + k, part].astype(f32), 0.0)
                 total[part, :, near] += jnp.where(lane_id >= shift, tile, 0.0)
                 total[part, :, far] += jnp.where(lane_id < shift, tile, 0.0)
     store = pltpu.make_async_copy(total, out_ref.at[:, 0], sem)
@@ -331,14 +325,15 @@
     anywhere = pl.BlockSpec(memory_space=pl.ANY)
     hbm = pl.BlockSpec(memory_space=pltpu.HBM)
     dma = pltpu.SemaphoreType.DMA
-    grads, info = pl.pallas_call(
+    coords = scan_coords.T
+    grads, theirs = pl.pallas_call(
         gather_kernel,
         out_shape=(
-            jax.ShapeDtypeStruct((2 * CAP, 2, N, N), bf16),
-            jax.ShapeDtypeStruct((2, CAP, 2), jnp.int32),
+            pltpu.VMEM((2 * CAP, 2, N, N), bf16),
+            pltpu.VMEM((2, CAP), jnp.int32),
         ),
         in_specs=[vmem, smem, hbm, hbm, hbm, hbm],
-        out_specs=(anywhere, vmem),
+        out_specs=(vmem, vmem),
         scratch_shapes=[
             pltpu.VMEM((NCOL // N, 2, N, N), f32),
             pltpu.VMEM((2, N, N), f32),
@@ -346,7 +341,7 @@
             pltpu.VMEM((N, N), f32),
             pltpu.VMEM((8, N), f32),
             pltpu.VMEM((8, N), f32),
-            pltpu.VMEM((CAP, 2), jnp.int32),
+            pltpu.VMEM((2, CAP), jnp.int32),
             pltpu.VMEM((CAP, 2, N, N), bf16),
             pltpu.VMEM((CAP, 2, N, N), bf16),
             pltpu.VMEM((SLICES, 2, N, N), bf16),
@@ -361,16 +356,16 @@
             collective_id=0, has_side_effects=True, vmem_limit_bytes=60 << 20
         ),
         name="chain",
-    )(scan_coords, scan_counts, object_field, probe_wave, measured, jnp.asarray(tables()))
+    )(coords, scan_counts, object_field, probe_wave, measured, jnp.asarray(tables()))
     return pl.pallas_call(
         scatter_kernel,
         out_shape=jax.ShapeDtypeStruct(object_field.shape, f32),
-        in_specs=[vmem, vmem],
+        in_specs=[vmem, vmem, vmem],
         out_specs=anywhere,
         scratch_shapes=[pltpu.VMEM((2, N, NCOL), f32), dma],
         compiler_params=pltpu.CompilerParams(vmem_limit_bytes=40 << 20),
         name="scatter",
-    )(info, grads)
+    )(coords, theirs, grads)
 
 
 def solution(mesh):

time: 40.9 us -> 37.1 us (0.907)
  local copies, waits for them, and re-layouts: 3.01 us -> 0.01 us
  Pallas kernels: 36.9 us -> 36.3 us
    unnamed x5 -> x2, local copies, waits for them, and re-layouts: 3.01 us -> 0.01 us
where the time goes in v1:
time: 37.1 us; the launch traced here: 37 us
  Pallas kernels  36.3 us (98%)
  between operations  0.68 us (2%)
    pallas_call x1, Pallas kernels, per_device(): pl.pallas_call(gather_kernel, out_shape=(pltpu.VMEM((2 * CAP, 2, N, N), b...  34.4 us
    pallas_call x1, Pallas kernels, per_device(): pl.pallas_call(scatter_kernel, out_shape=jax.ShapeDtypeStruct(object_fiel...  1.82 us

profile of v1, /device:TPU:1, one launch (start us, length us, event | category | flops | bytes accessed | tf_op | source)
XLA Modules:
  0.0 37.0 jit_solution(488378668394278523)
XLA Ops:
  0.0 0.0 copy-start
  0.7 34.4 %chain.1 = (bf16[6,2,128,128]{3,2,1,0:T(8,128)(2,1)S(1)}, s32[2,3]{1,0:T(2,128)S(1)}) custom-call(s32[2,3]{1,0:T(2,128)} %bitcast.1, s32[1]{0:T(128)S(6)} %copy.7.counts_ref, f32[2,1,128,2048]{3,2,1,0:T(8,128)} %object_ref.1, f32[2,128,128]{2,1,0:T(8,128)} %probe_ref.1, f32[3,128,128]{2,1,0:T(8,128)} %measured_ref.1, ...), custom_call_target="tpu_custom_call" | custom-call | tf_op jit(solution)/shard_map/chain/pallas_call | solution.py:329
  35.1 0.0 copy-done
  35.1 1.8 %scatter.1 = f32[2,1,128,2048]{3,2,1,0:T(8,128)} custom-call(s32[2,3]{1,0:T(2,128)S(1)} %bitcast.2, s32[2,3]{1,0:T(2,128)S(1)} %get-tuple-element.7.their_ref, bf16[6,2,128,128]{3,2,1,0:T(8,128)(2,1)S(1)} %get-tuple-element.8.grads_ref), custom_call_target="tpu_custom_call" | custom-call | tf_op jit(solution)/shard_map/scatter/pallas_call | solution.py:360
Async XLA Ops:
  0.0 35.1 %copy-start = (s32[3,2]{0,1:T(2,128)S(1)}, s32[3,2]{0,1:T(2,128)}, u32[]{:S(2)}) copy-start(s32[3,2]{0,1:T(2,128)} %param.8) | copy-start | bytes 76

commit v2 on v1

--- a/solution.py
+++ b/solution.py
@@ -12,7 +12,8 @@
 SLICES = 8
 CAP = 3
 NCOL = 2048
-WORKERS = (0, 2, 6)
+WORKERS = (0, 2, 4)
+ORDER = (2, 1, 0)
 MESH = pl.DeviceIdType.MESH
 
 
@@ -61,9 +62,9 @@
 
 
 def gather_kernel(
-    coords_ref, counts_ref, object_ref, probe_ref, measured_ref, tables_ref,
+    coords_hbm, counts_hbm, object_ref, probe_ref, measured_ref, tables_ref,
     grads_ref, info_ref,
-    strip, probe, table, sample, live, live_in, coords_in,
+    coords_ref, counts_ref, strip, probe, table, sample, live, live_in, coords_in,
     top_out, low_out, tops, lows, kept, grad_out,
     block_sem, load_sem, coord_sem, sample_sem, live_sem,
     top_send, top_recv, low_send, low_recv, grad_send, grad_recv, own_sem,
@@ -74,7 +75,34 @@
     after = lax.rem(p + 1, strips)
     before = lax.rem(p + strips - 1, strips)
     is_worker = (s == WORKERS[0]) | (s == WORKERS[1]) | (s == WORKERS[2])
-    slot = s // 2 - s // 6
+    slot = s // 2
+
+    load_coords = pltpu.make_async_copy(coords_hbm, coords_ref, load_sem.at[2])
+    load_counts = pltpu.make_async_copy(counts_hbm, counts_ref, load_sem.at[3])
+    load_coords.start()
+    barrier = pltpu.get_barrier_semaphore()
+
+    def greet(where):
+        pl.semaphore_signal(barrier, inc=1, device_id=where, device_id_type=MESH)
+
+    for w in WORKERS:
+        greet((w, after))
+
+        @pl.when(s != w)
+        def _():
+            greet((w, p))
+
+    @pl.when(is_worker)
+    def _():
+        for other in range(SLICES):
+            greet((other, before))
+
+            @pl.when(s != other)
+            def _():
+                greet((other, p))
+
+    greet((s, after))
+    greet((s, before))
 
     def load_block(c):
         columns = pl.ds(pl.multiple_of(c * N, N), N)
@@ -89,36 +117,14 @@
         return carry
 
     lax.fori_loop(0, NCOL // N, start_block, 0)
-    load_probe = pltpu.make_async_copy(probe_ref, probe, load_sem.at[1])
-    load_table = pltpu.make_async_copy(tables_ref, table, load_sem.at[2])
-
-    barrier = pltpu.get_barrier_semaphore()
-
-    def greet(where):
-        pl.semaphore_signal(barrier, inc=1, device_id=where, device_id_type=MESH)
-
-    greet((s, after))
-    greet((s, before))
-    for w in WORKERS:
-        greet((w, after))
-
-        @pl.when(s != w)
-        def _():
-            greet((w, p))
+    load_probe = pltpu.make_async_copy(probe_ref, probe, load_sem.at[0])
+    load_table = pltpu.make_async_copy(tables_ref, table, load_sem.at[1])
 
     @pl.when(is_worker)
     def _():
         load_probe.start()
         load_table.start()
-        for other in range(SLICES):
-            greet((other, before))
-
-            @pl.when(s != other)
-            def _():
-                greet((other, p))
-
-    @pl.when(is_worker)
-    def _():
+        load_counts.start()
         pl.semaphore_wait(barrier, 22)
 
     @pl.when(jnp.logical_not(is_worker))
@@ -132,20 +138,13 @@
         )
 
     coord_copy = send(coords_ref, coords_in, coord_sem.at[0], coord_sem.at[1], (s, after))
+    load_coords.wait()
     coord_copy.start()
 
     def sample_copy(k):
         return send(measured_ref.at[k], sample, sample_sem.at[0], sample_sem.at[1], (s, after))
 
     live_copy = send(live, live_in, live_sem.at[0], live_sem.at[1], (s, after))
-    for k, w in enumerate(WORKERS):
-
-        @pl.when(s == w)
-        def _():
-            sample_copy(k).start()
-            live[...] = jnp.clip(jnp.full((8, N), counts_ref[0] - k, jnp.int32), 0, 1).astype(f32)
-            live_copy.start()
-
     row_id = lax.broadcasted_iota(jnp.int32, (N, N), 0)
     lane_id = lax.broadcasted_iota(jnp.int32, (N, N), 1)
 
@@ -160,7 +159,8 @@
 
     lax.fori_loop(0, NCOL // N, wait_block, 0)
     own = coords_ref[...]
-    for k, w in enumerate(WORKERS):
+    for k in ORDER:
+        w = WORKERS[k]
         row, block, shift = corner(own, k, p)
         cut(row_id >= row, block, shift, top_out, k)
         send(top_out.at[k], tops.at[s], top_send.at[k], top_recv.at[s], (w, after)).start()
@@ -169,7 +169,8 @@
     theirs = coords_in[...]
     info_ref[...] = theirs
     corners = [corner(theirs, k, before) for k in range(CAP)]
-    for k, w in enumerate(WORKERS):
+    for k in ORDER:
+        w = WORKERS[k]
         row, block, shift = corners[k]
         cut(row_id < row, block, shift, low_out, k)
 
@@ -180,6 +181,18 @@
         @pl.when(s == w)
         def _():
             lows[s] = low_out[k]
+
+    @pl.when(is_worker)
+    def _():
+        load_counts.wait()
+
+    for k, w in enumerate(WORKERS):
+
+        @pl.when(s == w)
+        def _():
+            sample_copy(k).start()
+            live[...] = jnp.clip(jnp.full((8, N), counts_ref[0] - k, jnp.int32), 0, 1).astype(f32)
+            live_copy.start()
 
     @pl.when(is_worker)
     def _():
@@ -299,9 +312,9 @@
 def scatter_kernel(own_ref, their_ref, grads_ref, out_ref, total, sem):
     p = lax.axis_index("pos")
     before = lax.rem(p + lax.axis_size("pos") - 1, lax.axis_size("pos"))
-    total[...] = jnp.zeros((2, N, NCOL), f32)
     row_id = lax.broadcasted_iota(jnp.int32, (N, N), 0)
     lane_id = lax.broadcasted_iota(jnp.int32, (N, N), 1)
+    places = []
     for side in range(2):
         coords = own_ref[...] if side == 0 else their_ref[...]
         for k in range(CAP):
@@ -310,18 +323,22 @@
             base = pl.multiple_of(block * N, N)
             near = pl.ds(base, N)
             far = pl.ds(pl.multiple_of(base + N, N), N)
-            for part in range(2):
-                tile = jnp.where(keep, grads_ref[side * CAP + k, part].astype(f32), 0.0)
-                total[part, :, near] += jnp.where(lane_id >= shift, tile, 0.0)
-                total[part, :, far] += jnp.where(lane_id < shift, tile, 0.0)
-    store = pltpu.make_async_copy(total, out_ref.at[:, 0], sem)
-    store.start()
-    store.wait()
+            places.append((keep, near, far, shift))
+    stores = []
+    for part in range(2):
+        total[part] = jnp.zeros((N, NCOL), f32)
+        for tile_id, (keep, near, far, shift) in enumerate(places):
+            tile = jnp.where(keep, grads_ref[tile_id, part].astype(f32), 0.0)
+            total[part, :, near] += jnp.where(lane_id >= shift, tile, 0.0)
+            total[part, :, far] += jnp.where(lane_id < shift, tile, 0.0)
+        stores.append(pltpu.make_async_copy(total.at[part], out_ref.at[part, 0], sem.at[part]))
+        stores[-1].start()
+    for store in stores:
+        store.wait()
 
 
 def per_device(object_field, probe_wave, scan_coords, scan_counts, measured):
     vmem = pl.BlockSpec(memory_space=pltpu.VMEM)
-    smem = pl.BlockSpec(memory_space=pltpu.SMEM)
     anywhere = pl.BlockSpec(memory_space=pl.ANY)
     hbm = pl.BlockSpec(memory_space=pltpu.HBM)
     dma = pltpu.SemaphoreType.DMA
@@ -332,9 +349,11 @@
             pltpu.VMEM((2 * CAP, 2, N, N), bf16),
             pltpu.VMEM((2, CAP), jnp.int32),
         ),
-        in_specs=[vmem, smem, hbm, hbm, hbm, hbm],
+        in_specs=[hbm, hbm, hbm, hbm, hbm, hbm],
         out_specs=(vmem, vmem),
         scratch_shapes=[
+            pltpu.VMEM((2, CAP), jnp.int32),
+            pltpu.SMEM((1,), jnp.int32),
             pltpu.VMEM((NCOL // N, 2, N, N), f32),
             pltpu.VMEM((2, N, N), f32),
             pltpu.VMEM((4, 2 * N, 2 * N), bf16),
@@ -348,7 +367,7 @@
             pltpu.VMEM((SLICES, 2, N, N), bf16),
             pltpu.VMEM((SLICES, 2, N, N), f32),
             pltpu.VMEM((SLICES, 2, N, N), bf16),
-            dma((NCOL // N,)), dma((3,)), dma((2,)), dma((2,)), dma((2,)),
+            dma((NCOL // N,)), dma((4,)), dma((2,)), dma((2,)), dma((2,)),
             dma((CAP,)), dma((SLICES,)), dma((CAP,)), dma((SLICES,)),
             dma((SLICES, 2)), dma((2 * CAP,)), dma,
         ],
@@ -362,7 +381,7 @@
         out_shape=jax.ShapeDtypeStruct(object_field.shape, f32),
         in_specs=[vmem, vmem, vmem],
         out_specs=anywhere,
-        scratch_shapes=[pltpu.VMEM((2, N, NCOL), f32), dma],
+        scratch_shapes=[pltpu.VMEM((2, N, NCOL), f32), dma((2,))],
         compiler_params=pltpu.CompilerParams(vmem_limit_bytes=40 << 20),
         name="scatter",
     )(coords, theirs, grads)

time: 37.1 us -> 34 us (0.916)
  Pallas kernels: 36.3 us -> 33.2 us
    pallas_call x1, Pallas kernels: 34.4 us -> 31.6 us  [per_device(): pl.pallas_call(gather_kernel, out_shape=(pltpu.VMEM((2 * CAP, 2, N, N), b...]
where the time goes in v2:
time: 34 us; the launch traced here: 33.9 us
  Pallas kernels  33.2 us (98%)
  between operations  0.68 us (2%)
    pallas_call x1, Pallas kernels, per_device(): pl.pallas_call(gather_kernel, out_shape=(pltpu.VMEM((2 * CAP, 2, N, N), b...  31.6 us
    pallas_call x1, Pallas kernels, per_device(): pl.pallas_call(scatter_kernel, out_shape=jax.ShapeDtypeStruct(object_fiel...  1.63 us

profile of v2, /device:TPU:1, one launch (start us, length us, event | category | flops | bytes accessed | tf_op | source)
XLA Modules:
  0.0 33.9 jit_solution(13726519216885214030)
XLA Ops:
  0.0 0.0 copy-start
  0.7 31.6 %chain.1 = (bf16[6,2,128,128]{3,2,1,0:T(8,128)(2,1)S(1)}, s32[2,3]{1,0:T(2,128)S(1)}) custom-call(s32[2,3]{1,0:T(2,128)} %bitcast.1, s32[1]{0:T(128)S(6)} %copy.7.counts_hbm, f32[2,1,128,2048]{3,2,1,0:T(8,128)} %object_ref.1, f32[2,128,128]{2,1,0:T(8,128)} %probe_ref.1, f32[3,128,128]{2,1,0:T(8,128)} %measured_ref.1, ...), custom_call_target="tpu_custom_call" | custom-call | tf_op jit(solution)/shard_map/chain/pallas_call | solution.py:346
  32.2 0.0 copy-done
  32.2 1.6 %scatter.1 = f32[2,1,128,2048]{3,2,1,0:T(8,128)} custom-call(s32[2,3]{1,0:T(2,128)S(1)} %bitcast.2, s32[2,3]{1,0:T(2,128)S(1)} %get-tuple-element.7.their_ref, bf16[6,2,128,128]{3,2,1,0:T(8,128)(2,1)S(1)} %get-tuple-element.8.grads_ref), custom_call_target="tpu_custom_call" | custom-call | tf_op jit(solution)/shard_map/scatter/pallas_call | solution.py:379
Async XLA Ops:
  0.0 32.2 %copy-start = (s32[3,2]{0,1:T(2,128)S(1)}, s32[3,2]{0,1:T(2,128)}, u32[]{:S(2)}) copy-start(s32[3,2]{0,1:T(2,128)} %param.8) | copy-start | bytes 76

commit v3 on v2

--- a/solution.py
+++ b/solution.py
@@ -14,6 +14,7 @@
 NCOL = 2048
 WORKERS = (0, 2, 4)
 ORDER = (2, 1, 0)
+DIRECT = 7
 MESH = pl.DeviceIdType.MESH
 
 
@@ -41,17 +42,19 @@
 def sandwich(left, right, real, imag, sign):
     x = jnp.concatenate([real.astype(bf16), imag.astype(bf16)], axis=1)
     x = jnp.concatenate([x, x], axis=0)
-    y = jnp.dot(left, x, preferred_element_type=f32)
+    a = jnp.dot(left[:N], x, preferred_element_type=f32)
+    b = jnp.dot(left[N:], x, preferred_element_type=f32)
     if sign > 0:
-        real, imag = y[:N, :N] - y[N:, N:], y[:N, N:] + y[N:, :N]
+        real, imag = a[:, :N] - b[:, N:], a[:, N:] + b[:, :N]
     else:
-        real, imag = y[:N, :N] + y[N:, N:], y[:N, N:] - y[N:, :N]
-    x = jnp.concatenate([real.astype(bf16), imag.astype(bf16)], axis=0)
-    x = jnp.concatenate([x, x], axis=1)
-    y = jnp.dot(x, right, preferred_element_type=f32)
+        real, imag = a[:, :N] + b[:, N:], a[:, N:] - b[:, :N]
+    real = real.astype(bf16)
+    imag = imag.astype(bf16)
+    a = jnp.dot(jnp.concatenate([real, real], axis=1), right, preferred_element_type=f32)
+    b = jnp.dot(jnp.concatenate([imag, imag], axis=1), right, preferred_element_type=f32)
     if sign > 0:
-        return y[:N, :N] - y[N:, N:], y[:N, N:] + y[N:, :N]
-    return y[:N, :N] + y[N:, N:], y[N:, :N] - y[:N, N:]
+        return a[:, :N] - b[:, N:], a[:, N:] + b[:, :N]
+    return a[:, :N] + b[:, N:], b[:, :N] - a[:, N:]
 
 
 def corner(coords, k, strip):
@@ -67,7 +70,7 @@
     coords_ref, counts_ref, strip, probe, table, sample, live, live_in, coords_in,
     top_out, low_out, tops, lows, kept, grad_out,
     block_sem, load_sem, coord_sem, sample_sem, live_sem,
-    top_send, top_recv, low_send, low_recv, grad_send, grad_recv, own_sem,
+    top_send, top_recv, low_send, low_recv, grad_send, grad_recv, own_sem, relay_send,
 ):
     s = lax.axis_index("slab")
     p = lax.axis_index("pos")
@@ -242,9 +245,13 @@
             real, imag = moved
             grad_out[i, 0] = (kept[i, 0] * real + kept[i, 1] * imag).astype(bf16)
             grad_out[i, 1] = (kept[i, 0] * imag - kept[i, 1] * real).astype(bf16)
-            send(
-                grad_out.at[i], grads_ref.at[slot], grad_send.at[i, 0], grad_recv.at[slot], (i, before)
-            ).start()
+
+            @pl.when(i < DIRECT)
+            def _():
+                send(
+                    grad_out.at[i], grads_ref.at[slot], grad_send.at[i, 0], grad_recv.at[slot],
+                    (i, before),
+                ).start()
 
             @pl.when(i != s)
             def _():
@@ -271,15 +278,31 @@
 
         emit(0, lax.fori_loop(0, SLICES - 1, backward, moved))
 
+    here = grad_out.at[0]
+
+    def grad_wait(place):
+        send(here, grads_ref.at[place], grad_send.at[0, 0], grad_recv.at[place], (s, after)).wait_recv()
+
+    def relay(k):
+        return send(
+            grads_ref.at[CAP + k], grads_ref.at[k], relay_send.at[k], grad_recv.at[k], (s, before)
+        )
+
+    @pl.when(s >= DIRECT)
+    def _():
+        for k in ORDER:
+            grad_wait(CAP + k)
+            relay(k).start()
+
     for k, w in enumerate(WORKERS):
-        here = grad_out.at[0]
-        send(here, grads_ref.at[k], grad_send.at[0, 0], grad_recv.at[k], (s, after)).wait_recv()
+        grad_wait(k)
+
+        @pl.when((s != w) & (s < DIRECT))
+        def _():
+            grad_wait(CAP + k)
 
         @pl.when(s != w)
         def _():
-            send(
-                here, grads_ref.at[CAP + k], grad_send.at[0, 0], grad_recv.at[CAP + k], (s, after)
-            ).wait_recv()
             send(low_out.at[k], lows.at[s], low_send.at[k], low_recv.at[s], (w, p)).wait_send()
 
         @pl.when(s == w)
@@ -290,12 +313,22 @@
 
         send(top_out.at[k], tops.at[s], top_send.at[k], top_recv.at[s], (w, after)).wait_send()
 
+    @pl.when(s >= DIRECT)
+    def _():
+        for k in range(CAP):
+            relay(k).wait_send()
+
     coord_copy.wait_send()
 
     @pl.when(is_worker)
     def _():
         def drain(i, carry):
-            send(grad_out.at[i], grads_ref.at[slot], grad_send.at[i, 0], grad_recv.at[slot], (i, before)).wait_send()
+            @pl.when(i < DIRECT)
+            def _():
+                send(
+                    grad_out.at[i], grads_ref.at[slot], grad_send.at[i, 0], grad_recv.at[slot],
+                    (i, before),
+                ).wait_send()
 
             @pl.when(i != s)
             def _():
@@ -369,7 +402,7 @@
             pltpu.VMEM((SLICES, 2, N, N), bf16),
             dma((NCOL // N,)), dma((4,)), dma((2,)), dma((2,)), dma((2,)),
             dma((CAP,)), dma((SLICES,)), dma((CAP,)), dma((SLICES,)),
-            dma((SLICES, 2)), dma((2 * CAP,)), dma,
+            dma((SLICES, 2)), dma((2 * CAP,)), dma, dma((CAP,)),
         ],
         compiler_params=pltpu.CompilerParams(
             collective_id=0, has_side_effects=True, vmem_limit_bytes=60 << 20

time: 34 us -> 33.2 us (0.976)
  Pallas kernels: 33.2 us -> 32.4 us
    pallas_call x1, Pallas kernels: 31.6 us -> 30.8 us  [per_device(): pl.pallas_call(gather_kernel, out_shape=(pltpu.VMEM((2 * CAP, 2, N, N), b...]
where the time goes in v3:
time: 33.2 us; the launch traced here: 33.1 us
  Pallas kernels  32.4 us (98%)
  between operations  0.68 us (2%)
    pallas_call x1, Pallas kernels, per_device(): pl.pallas_call(gather_kernel, out_shape=(pltpu.VMEM((2 * CAP, 2, N, N), b...  30.8 us
    pallas_call x1, Pallas kernels, per_device(): pl.pallas_call(scatter_kernel, out_shape=jax.ShapeDtypeStruct(object_fiel...  1.63 us

profile of v3, /device:TPU:1, one launch (start us, length us, event | category | flops | bytes accessed | tf_op | source)
XLA Modules:
  0.0 33.1 jit_solution(12599956355554082195)
XLA Ops:
  0.0 0.0 copy-start
  0.7 30.8 %chain.1 = (bf16[6,2,128,128]{3,2,1,0:T(8,128)(2,1)S(1)}, s32[2,3]{1,0:T(2,128)S(1)}) custom-call(s32[2,3]{1,0:T(2,128)} %bitcast.1, s32[1]{0:T(128)S(6)} %copy.7.counts_hbm, f32[2,1,128,2048]{3,2,1,0:T(8,128)} %object_ref.1, f32[2,128,128]{2,1,0:T(8,128)} %probe_ref.1, f32[3,128,128]{2,1,0:T(8,128)} %measured_ref.1, ...), custom_call_target="tpu_custom_call" | custom-call | tf_op jit(solution)/shard_map/chain/pallas_call | solution.py:379
  31.4 0.0 copy-done
  31.5 1.6 %scatter.1 = f32[2,1,128,2048]{3,2,1,0:T(8,128)} custom-call(s32[2,3]{1,0:T(2,128)S(1)} %bitcast.2, s32[2,3]{1,0:T(2,128)S(1)} %get-tuple-element.7.their_ref, bf16[6,2,128,128]{3,2,1,0:T(8,128)(2,1)S(1)} %get-tuple-element.8.grads_ref), custom_call_target="tpu_custom_call" | custom-call | tf_op jit(solution)/shard_map/scatter/pallas_call | solution.py:412
Async XLA Ops:
  0.0 31.4 %copy-start = (s32[3,2]{0,1:T(2,128)S(1)}, s32[3,2]{0,1:T(2,128)}, u32[]{:S(2)}) copy-start(s32[3,2]{0,1:T(2,128)} %param.8) | copy-start | bytes 76

commit v4 on v3

--- a/solution.py
+++ b/solution.py
@@ -88,12 +88,7 @@
     def greet(where):
         pl.semaphore_signal(barrier, inc=1, device_id=where, device_id_type=MESH)
 
-    for w in WORKERS:
-        greet((w, after))
-
-        @pl.when(s != w)
-        def _():
-            greet((w, p))
+    greet((s, before))
 
     @pl.when(is_worker)
     def _():
@@ -103,9 +98,6 @@
             @pl.when(s != other)
             def _():
                 greet((other, p))
-
-    greet((s, after))
-    greet((s, before))
 
     def load_block(c):
         columns = pl.ds(pl.multiple_of(c * N, N), N)
@@ -128,11 +120,11 @@
         load_probe.start()
         load_table.start()
         load_counts.start()
-        pl.semaphore_wait(barrier, 22)
+        pl.semaphore_wait(barrier, 6)
 
     @pl.when(jnp.logical_not(is_worker))
     def _():
-        pl.semaphore_wait(barrier, 8)
+        pl.semaphore_wait(barrier, 7)
 
     def send(src, dst, send_sem, recv_sem, where):
         return pltpu.make_async_remote_copy(

time: 33.2 us -> 32.3 us (0.973)
  Pallas kernels: 32.4 us -> 31.3 us
    pallas_call x1, Pallas kernels: 30.8 us -> 29.6 us  [per_device(): pl.pallas_call(gather_kernel, out_shape=(pltpu.VMEM((2 * CAP, 2, N, N), b...]
where the time goes in v4:
time: 32.3 us; the launch traced here: 31.9 us
  Pallas kernels  31.3 us (97%)
  between operations  0.68 us (2%)
    pallas_call x1, Pallas kernels, per_device(): pl.pallas_call(gather_kernel, out_shape=(pltpu.VMEM((2 * CAP, 2, N, N), b...  29.6 us
    pallas_call x1, Pallas kernels, per_device(): pl.pallas_call(scatter_kernel, out_shape=jax.ShapeDtypeStruct(object_fiel...  1.63 us

profile of v4, /device:TPU:1, one launch (start us, length us, event | category | flops | bytes accessed | tf_op | source)
XLA Modules:
  0.0 31.9 jit_solution(2424104397923224094)
XLA Ops:
  0.0 0.0 copy-start
  0.7 29.6 %chain.1 = (bf16[6,2,128,128]{3,2,1,0:T(8,128)(2,1)S(1)}, s32[2,3]{1,0:T(2,128)S(1)}) custom-call(s32[2,3]{1,0:T(2,128)} %bitcast.1, s32[1]{0:T(128)S(6)} %copy.7.counts_hbm, f32[2,1,128,2048]{3,2,1,0:T(8,128)} %object_ref.1, f32[2,128,128]{2,1,0:T(8,128)} %probe_ref.1, f32[3,128,128]{2,1,0:T(8,128)} %measured_ref.1, ...), custom_call_target="tpu_custom_call" | custom-call | tf_op jit(solution)/shard_map/chain/pallas_call | solution.py:371
  30.3 0.0 copy-done
  30.3 1.6 %scatter.1 = f32[2,1,128,2048]{3,2,1,0:T(8,128)} custom-call(s32[2,3]{1,0:T(2,128)S(1)} %bitcast.2, s32[2,3]{1,0:T(2,128)S(1)} %get-tuple-element.7.their_ref, bf16[6,2,128,128]{3,2,1,0:T(8,128)(2,1)S(1)} %get-tuple-element.8.grads_ref), custom_call_target="tpu_custom_call" | custom-call | tf_op jit(solution)/shard_map/scatter/pallas_call | solution.py:404
Async XLA Ops:
  0.0 30.3 %copy-start = (s32[3,2]{0,1:T(2,128)S(1)}, s32[3,2]{0,1:T(2,128)}, u32[]{:S(2)}) copy-start(s32[3,2]{0,1:T(2,128)} %param.8) | copy-start | bytes 76

commit v5 on v4

--- a/solution.py
+++ b/solution.py
@@ -12,7 +12,7 @@
 SLICES = 8
 CAP = 3
 NCOL = 2048
-WORKERS = (0, 2, 4)
+WORKERS = (0, 3, 5)
 ORDER = (2, 1, 0)
 DIRECT = 7
 MESH = pl.DeviceIdType.MESH

time: 32.3 us -> 31.3 us (0.969)
  the two profiles are of different devices: /device:TPU:1 before, /device:TPU:248 now
where the time goes in v5:
time: 31.3 us; the launch traced here: 31.2 us
  Pallas kernels  30.5 us (97%)
  between operations  0.68 us (2%)
    pallas_call x1, Pallas kernels, per_device(): pl.pallas_call(gather_kernel, out_shape=(pltpu.VMEM((2 * CAP, 2, N, N), b...  28.9 us
    pallas_call x1, Pallas kernels, per_device(): pl.pallas_call(scatter_kernel, out_shape=jax.ShapeDtypeStruct(object_fiel...  1.63 us

profile of v5, /device:TPU:248, one launch (start us, length us, event | category | flops | bytes accessed | tf_op | source)
XLA Modules:
  0.0 31.2 jit_solution(12918983200362403219)
XLA Ops:
  0.0 0.0 copy-start
  0.7 28.9 %chain.1 = (bf16[6,2,128,128]{3,2,1,0:T(8,128)(2,1)S(1)}, s32[2,3]{1,0:T(2,128)S(1)}) custom-call(s32[2,3]{1,0:T(2,128)} %bitcast.1, s32[1]{0:T(128)S(6)} %copy.7.counts_hbm, f32[2,1,128,2048]{3,2,1,0:T(8,128)} %object_ref.1, f32[2,128,128]{2,1,0:T(8,128)} %probe_ref.1, f32[3,128,128]{2,1,0:T(8,128)} %measured_ref.1, ...), custom_call_target="tpu_custom_call" | custom-call | tf_op jit(solution)/shard_map/chain/pallas_call | solution.py:371
  29.5 0.0 copy-done
  29.5 1.6 %scatter.1 = f32[2,1,128,2048]{3,2,1,0:T(8,128)} custom-call(s32[2,3]{1,0:T(2,128)S(1)} %bitcast.2, s32[2,3]{1,0:T(2,128)S(1)} %get-tuple-element.7.their_ref, bf16[6,2,128,128]{3,2,1,0:T(8,128)(2,1)S(1)} %get-tuple-element.8.grads_ref), custom_call_target="tpu_custom_call" | custom-call | tf_op jit(solution)/shard_map/scatter/pallas_call | solution.py:404
Async XLA Ops:
  0.0 29.5 %copy-start = (s32[3,2]{0,1:T(2,128)S(1)}, s32[3,2]{0,1:T(2,128)}, u32[]{:S(2)}) copy-start(s32[3,2]{0,1:T(2,128)} %param.8) | copy-start | bytes 76

commit v6 on v5

--- a/solution.py
+++ b/solution.py
@@ -12,9 +12,9 @@
 SLICES = 8
 CAP = 3
 NCOL = 2048
-WORKERS = (0, 3, 5)
+WORKERS = (0, 3, 7)
 ORDER = (2, 1, 0)
-DIRECT = 7
+RELAYED = 5
 MESH = pl.DeviceIdType.MESH
 
 
@@ -78,7 +78,7 @@
     after = lax.rem(p + 1, strips)
     before = lax.rem(p + strips - 1, strips)
     is_worker = (s == WORKERS[0]) | (s == WORKERS[1]) | (s == WORKERS[2])
-    slot = s // 2
+    slot = s // 3
 
     load_coords = pltpu.make_async_copy(coords_hbm, coords_ref, load_sem.at[2])
     load_counts = pltpu.make_async_copy(counts_hbm, counts_ref, load_sem.at[3])
@@ -238,18 +238,18 @@
             grad_out[i, 0] = (kept[i, 0] * real + kept[i, 1] * imag).astype(bf16)
             grad_out[i, 1] = (kept[i, 0] * imag - kept[i, 1] * real).astype(bf16)
 
-            @pl.when(i < DIRECT)
+            @pl.when(i != s)
+            def _():
+                send(
+                    grad_out.at[i], grads_ref.at[CAP + slot], grad_send.at[i, 1],
+                    grad_recv.at[CAP + slot], (i, p),
+                ).start()
+
+            @pl.when(i != RELAYED)
             def _():
                 send(
                     grad_out.at[i], grads_ref.at[slot], grad_send.at[i, 0], grad_recv.at[slot],
                     (i, before),
-                ).start()
-
-            @pl.when(i != s)
-            def _():
-                send(
-                    grad_out.at[i], grads_ref.at[CAP + slot], grad_send.at[i, 1],
-                    grad_recv.at[CAP + slot], (i, p),
                 ).start()
 
             @pl.when(i == s)
@@ -280,7 +280,7 @@
             grads_ref.at[CAP + k], grads_ref.at[k], relay_send.at[k], grad_recv.at[k], (s, before)
         )
 
-    @pl.when(s >= DIRECT)
+    @pl.when(s == RELAYED)
     def _():
         for k in ORDER:
             grad_wait(CAP + k)
@@ -289,7 +289,7 @@
     for k, w in enumerate(WORKERS):
         grad_wait(k)
 
-        @pl.when((s != w) & (s < DIRECT))
+        @pl.when((s != w) & (s != RELAYED))
         def _():
             grad_wait(CAP + k)
 
@@ -305,7 +305,7 @@
 
         send(top_out.at[k], tops.at[s], top_send.at[k], top_recv.at[s], (w, after)).wait_send()
 
-    @pl.when(s >= DIRECT)
+    @pl.when(s == RELAYED)
     def _():
         for k in range(CAP):
             relay(k).wait_send()
@@ -315,7 +315,7 @@
     @pl.when(is_worker)
     def _():
         def drain(i, carry):
-            @pl.when(i < DIRECT)
+            @pl.when(i != RELAYED)
             def _():
                 send(
                     grad_out.at[i], grads_ref.at[slot], grad_send.at[i, 0], grad_recv.at[slot],

time: 31.3 us -> 31 us (level)
  the two profiles are of different devices: /device:TPU:248 before, /device:TPU:2 now
where the time goes in v6:
time: 31 us; the launch traced here: 30.9 us
  Pallas kernels  30.2 us (97%)
  between operations  0.68 us (2%)
    pallas_call x1, Pallas kernels, per_device(): pl.pallas_call(gather_kernel, out_shape=(pltpu.VMEM((2 * CAP, 2, N, N), b...  28.6 us
    pallas_call x1, Pallas kernels, per_device(): pl.pallas_call(scatter_kernel, out_shape=jax.ShapeDtypeStruct(object_fiel...  1.63 us

profile of v6, /device:TPU:2, one launch (start us, length us, event | category | flops | bytes accessed | tf_op | source)
XLA Modules:
  0.0 30.9 jit_solution(15362078823099608439)
XLA Ops:
  0.0 0.0 copy-start
  0.7 28.6 %chain.1 = (bf16[6,2,128,128]{3,2,1,0:T(8,128)(2,1)S(1)}, s32[2,3]{1,0:T(2,128)S(1)}) custom-call(s32[2,3]{1,0:T(2,128)} %bitcast.1, s32[1]{0:T(128)S(6)} %copy.7.counts_hbm, f32[2,1,128,2048]{3,2,1,0:T(8,128)} %object_ref.1, f32[2,128,128]{2,1,0:T(8,128)} %probe_ref.1, f32[3,128,128]{2,1,0:T(8,128)} %measured_ref.1, ...), custom_call_target="tpu_custom_call" | custom-call | tf_op jit(solution)/shard_map/chain/pallas_call | solution.py:371
  29.3 0.0 copy-done
  29.3 1.6 %scatter.1 = f32[2,1,128,2048]{3,2,1,0:T(8,128)} custom-call(s32[2,3]{1,0:T(2,128)S(1)} %bitcast.2, s32[2,3]{1,0:T(2,128)S(1)} %get-tuple-element.7.their_ref, bf16[6,2,128,128]{3,2,1,0:T(8,128)(2,1)S(1)} %get-tuple-element.8.grads_ref), custom_call_target="tpu_custom_call" | custom-call | tf_op jit(solution)/shard_map/scatter/pallas_call | solution.py:404
Async XLA Ops:
  0.0 29.3 %copy-start = (s32[3,2]{0,1:T(2,128)S(1)}, s32[3,2]{0,1:T(2,128)}, u32[]{:S(2)}) copy-start(s32[3,2]{0,1:T(2,128)} %param.8) | copy-start | bytes 76
